TPU v7x, 32 devices: a whole 2x2x4 slice. The times are simulated.
32 devices in a mesh: row: 4 (over y, x), col: 8 (over z, core).
Axes of the slice: x: 2, y: 2, z: 4, core: 2. Of those that a mesh axis runs over, the one named last changes fastest.
Arguments:
- features: bfloat16 [16384, 256], P(('col', 'row')), may hold values from -6 to 6
- weight: bfloat16 [256, 256], replicated, may hold values from -0.375 to 0.375
- adjacency: int32 [64, 16, 256, 256], P('row', 'col'), may hold values 0 or 1
- tile_cols: int32 [64, 16], P('row', 'col'), may hold values from 0 to 7
- tile_counts: int32 [64, 8], P('row', 'col'), may hold values from 0 to 2
- cotangent: bfloat16 [16384, 256], P(('row', 'col')), may hold values from -6 to 6
Outputs:
- output: bfloat16 [16384, 256], P(('row', 'col'))
- feature_grad: bfloat16 [16384, 256], P(('col', 'row'))
- weight_grad: float32 [256, 256], replicated
Inputs may be any that keep to these rules, and one draw needn't show every extreme that they name: `tile_counts`: slots of a block row at or after its count are not part of the graph.
All inputs are finite; a program needn't handle non-finite values. No bound on the sum of `adjacency` on one device may be relied on, other than what follows from the above.
Results may differ from a plain program's by a relative error of at most 0.0061.
Values may be sent and summed in bfloat16 or wider, within the bound.
A program may use at most 128 MiB of HBM per device.

v0:
```python
import math

import jax
import jax.numpy as jnp
from jax import lax
from jax.sharding import PartitionSpec as P


def shards(features, weight, adjacency, tile_cols, tile_counts, cotangent):
    block_rows = adjacency.shape[0]
    slot_count = adjacency.shape[1]
    tile_len = adjacency.shape[2]
    feat_width = features.shape[1]
    own_rows = features.shape[0]
    counts = tile_counts[:, 0]
    usable = jnp.arange(slot_count)[None, :] < counts[:, None]
    col_inputs = lax.all_gather(features, "row", axis=0, tiled=True)
    col_hidden = jnp.dot(col_inputs, weight, preferred_element_type=jnp.float32).astype(
        jnp.bfloat16
    )
    col_blocks = col_hidden.shape[0] // tile_len
    blocks = col_hidden.reshape(col_blocks, tile_len, feat_width)
    panels = jnp.take(blocks, tile_cols, axis=0)
    panels = jnp.where(usable[:, :, None, None], panels, jnp.zeros((), jnp.bfloat16))
    tile_bf = adjacency.astype(jnp.bfloat16)
    partial_value = jnp.einsum(
        "bkij,bkjf->bif", tile_bf, panels, preferred_element_type=jnp.float32
    )
    partial_value = partial_value.reshape(block_rows * tile_len, feat_width)
    row_sums = jnp.sum(adjacency, axis=3)
    row_degree = (
        jnp.sum(jnp.where(usable[:, :, None], row_sums, 0), axis=1).astype(jnp.float32).reshape(-1)
    )
    degree = lax.psum_scatter(row_degree, "col", scatter_dimension=0, tiled=True)
    summed = lax.psum_scatter(partial_value, "col", scatter_dimension=0, tiled=True)
    inv_root = lax.rsqrt(jnp.float32(1.0) + degree)[:, None]
    preact = summed * inv_root
    output = jax.nn.silu(preact).astype(jnp.bfloat16)
    sigmoid_v = jax.nn.sigmoid(preact)
    grad_sum = (
        cotangent.astype(jnp.float32) * sigmoid_v * (1.0 + preact * (1.0 - sigmoid_v)) * inv_root
    ).astype(jnp.bfloat16)
    grad_slab = lax.all_gather(grad_sum, "col", axis=0, tiled=True).reshape(
        block_rows, tile_len, feat_width
    )
    contribs = jnp.einsum("bkij,bif->bkjf", tile_bf, grad_slab, preferred_element_type=jnp.float32)
    onehot = (
        (tile_cols[:, :, None] == jnp.arange(col_blocks)[None, None, :]) & usable[:, :, None]
    ).astype(jnp.float32)
    col_partial = jnp.einsum("bkc,bkjf->cjf", onehot, contribs, precision=lax.Precision.HIGHEST)
    col_partial = col_partial.reshape(col_blocks * tile_len, feat_width)
    node_grad = lax.psum_scatter(col_partial, "row", scatter_dimension=0, tiled=True).astype(
        jnp.bfloat16
    )
    feature_grad = jnp.dot(node_grad, weight.T, preferred_element_type=jnp.float32).astype(
        jnp.bfloat16
    )
    node_total = own_rows * lax.axis_size("row") * lax.axis_size("col")
    weight_terms = jnp.dot(features.T, node_grad, preferred_element_type=jnp.float32)
    weight_grad = lax.psum(weight_terms, ("row", "col")) * jnp.float32(1.0 / math.sqrt(node_total))
    return (output, feature_grad, weight_grad)


def solution(mesh):
    placed = (
        P(("col", "row"), None),
        P(),
        P("row", "col", None, None),
        P("row", "col"),
        P("row", "col"),
        P(("row", "col"), None),
    )
    return jax.shard_map(
        shards,
        mesh=mesh,
        in_specs=placed,
        out_specs=(P(("row", "col"), None), P(("col", "row"), None), P()),
        check_vma=False,
    )
```

profile of v0, /device:TPU:0, one launch (start us, length us, event | category | flops | bytes accessed | tf_op | source)
XLA Modules:
  0.0 333.3 jit_solution(11807054258820807927)
XLA Ops:
  7.2 0.7 all-gather.3.cloned.1.call-update
  8.0 0.7 compare_and_fusion
  8.7 0.7 compare_select_fusion
  9.6 0.7 iota_compare_fusion.1
  10.4 28.9 %all-gather.3.cloned.1.call-done = bf16[2048,256]{1,0:T(8,128)(2,1)} async-done(((bf16[512,256]{1,0:T(8,128)(2,1)}), bf16[2048,256]{1,0:T(8,128)(2,1)}) %all-gather.3.cloned.1.call-update) | async-done | bytes 1048592 | tf_op jit(solution)/shard_map/all_gather | solution.py:17
  39.2 1.6 convolution_convert_fusion
  40.9 2.8 gather_fusion
  43.7 7.9 %fusion = f32[16,256,256,1]{1,2,3,0:T(8,128)} fusion(bf16[16,2,256,256]{3,2,1,0:T(8,128)(2,1)} %bitcast.36, pred[16,2]{1,0:T(8,128)(4,1)S(1)} %copy.42, pred[16,2]{1,0:T(8,128)(4,1)S(1)} %iota_compare_fusion.1, s32[16,2,256,256]{3,2,1,0:T(8,128)} %param.8), kind=kOutput, calls=%fused_computation.1 | convolution fusion | flops 1080033280 | bytes 16777280 | tf_op jit(solution)/shard_map/bkij,bkjf->bif/dot_general | solution.py:26
  51.7 4.6 %reduce_sum.18 = s32[16,2,256]{2,1,0:T(2,128)S(1)} reduce(s32[16,2,256,256]{3,2,1,0:T(8,128)} %param.8, s32[]{:T(128)} %constant.7.clone.1), dimensions={3}, to_apply=%region_1.2 | reduce | flops 2088960 | bytes 8421380 | tf_op jit(solution)/shard_map/reduce_sum | solution.py:30
  56.5 0.6 dynamic-slice
  57.7 30.4 %all-reduce = f32[4096]{0:T(1024)S(1)} all-reduce(f32[4096]{0:T(1024)S(1)} %bitcast.40), channel_id=3, replica_groups=mesh['row'=4,'col'=8] {'col'}, use_global_device_ids=true, to_apply=%region_3.4.clone | all-reduce | flops 4096 | bytes 32768
  88.2 14.2 %reduce-scatter.3.cloned.1.call-done = f32[512,256]{1,0:T(8,128)} async-done(((f32[4096,256]{1,0:T(8,128)}), f32[512,256]{1,0:T(8,128)}) %reduce-scatter.3.cloned.1.call-update) | async-done | bytes 524304 | tf_op jit(solution)/shard_map/reduce_scatter | solution.py:35
  102.4 2.2 multiply_convert_fusion
  104.7 27.2 %all-gather.5.cloned.1.call-done = bf16[4096,256]{1,0:T(8,128)(2,1)} async-done(((bf16[512,256]{1,0:T(8,128)(2,1)}), bf16[4096,256]{1,0:T(8,128)(2,1)}) %all-gather.5.cloned.1.call-update) | async-done | bytes 2097168 | tf_op jit(solution)/shard_map/all_gather | solution.py:43
  132.0 8.5 %convolution_bitcast_fusion = f32[16,2,256,256]{2,3,1,0:T(8,128)} fusion(bf16[16,256,256,1]{2,1,3,0:T(8,128)(2,1)} %bitcast.39, s32[16,2,256,256]{3,2,1,0:T(8,128)} %param.8), kind=kOutput, calls=%fused_computation.6 | convolution fusion | flops 1075838976 | bytes 18874368 | tf_op jit(solution)/shard_map/bkij,bif->bkjf/dot_general | solution.py:46
  140.5 10.5 %copy.47 = f32[16,2,256,256]{3,0,1,2:T(8,128)} copy(f32[16,2,256,256]{2,3,1,0:T(8,128)} %convolution_bitcast_fusion) | data formatting | bytes 16777216 | tf_op jit(solution)/shard_map/bkij,bif->bkjf/dot_general | solution.py:46
  151.0 5.2 %convolution_bitcast_fusion.1 = f32[8,256,256]{2,0,1:T(8,128)S(1)} fusion(f32[16,2,256,256]{3,0,1,2:T(8,128)} %copy.47, s32[16,2]{0,1:T(2,128)S(1)} %copy-done.3, pred[16,2]{0,1:T(4,128)(4,1)S(1)} %copy.45), kind=kOutput, calls=%fused_computation.12 | convolution fusion | flops 201327104 | bytes 10485920 | tf_op jit(solution)/shard_map/bkc,bkjf->cjf/dot_general | solution.py:50
  156.3 2.0 copy.48
  158.3 34.8 %reduce-scatter.5.cloned.1.call-done = f32[512,256]{1,0:T(8,128)} async-done(((f32[2048,256]{1,0:T(8,128)}), f32[512,256]{1,0:T(8,128)}) %reduce-scatter.5.cloned.1.call-update) | async-done | bytes 524304 | tf_op jit(solution)/shard_map/reduce_scatter | solution.py:52
  193.1 2.0 convolution_bitcast_fusion.2
  195.2 2.0 convolution_convert_fusion.1
  197.2 127.8 %all-reduce.3.cloned.1.call-done = f32[256,256]{0,1:T(8,128)} async-done(((f32[256,256]{0,1:T(8,128)}), f32[256,256]{0,1:T(8,128)}) %all-reduce.3.cloned.1.call-update) | async-done | bytes 262160 | tf_op jit(solution)/shard_map/psum | solution.py:60
  325.0 1.0 broadcast_multiply_fusion
  326.0 0.8 copy.49
  (28 shorter events, 0.9 us)
Async XLA Ops:
  7.2 32.1 %copy-start = (bf16[256,256]{1,0:T(8,128)(2,1)S(1)}, bf16[256,256]{1,0:T(8,128)(2,1)}, u32[]{:S(2)}) copy-start(bf16[256,256]{1,0:T(8,128)(2,1)} %param.7) | copy-start | bytes 393220
  7.2 32.0 %all-gather.3.cloned.1.call-start = ((), (), s32[]{:S(2)}) async-start(), calls=%async_computation.2 | async-start | bytes 1310720 | tf_op jit(solution)/shard_map/all_gather | solution.py:17
  7.9 94.5 %reduce-scatter.3.cloned.1.call-start = ((), (), s32[]{:S(2)}) async-start(), calls=%async_computation.3 | async-start | bytes 4718592 | tf_op jit(solution)/shard_map/reduce_scatter | solution.py:35
  51.6 80.4 %all-gather.5.cloned.1.call-start = ((), (), s32[]{:S(2)}) async-start(), calls=%async_computation.4 | async-start | bytes 2359296 | tf_op jit(solution)/shard_map/all_gather | solution.py:43
  51.7 4.8 %copy-start.4 = (u32[32]{0:T(128)S(1)}, u32[32]{0:T(128)}, u32[]{:S(2)}) copy-start(u32[32]{0:T(128)} %constant.31) | copy-start | bytes 388
  51.7 50.7 %copy-start.2 = (bf16[512,256]{1,0:T(8,128)(2,1)S(1)}, bf16[512,256]{1,0:T(8,128)(2,1)}, u32[]{:S(2)}) copy-start(bf16[512,256]{1,0:T(8,128)(2,1)} %param.11) | copy-start | bytes 786436
  104.6 88.5 %reduce-scatter.5.cloned.1.call-start = ((), (), s32[]{:S(2)}) async-start(), calls=%async_computation.5 | async-start | bytes 2621440 | tf_op jit(solution)/shard_map/reduce_scatter | solution.py:52
  140.5 10.5 %copy-start.3 = (s32[16,2]{0,1:T(2,128)S(1)}, s32[16,2]{0,1:T(2,128)}, u32[]{:S(2)}) copy-start(s32[16,2]{0,1:T(2,128)} %param.9) | copy-start | bytes 388
  156.3 36.9 %copy-start.1 = (bf16[512,256]{1,0:T(8,128)(2,1)S(1)}, bf16[512,256]{1,0:T(8,128)(2,1)}, u32[]{:S(2)}) copy-start(bf16[512,256]{1,0:T(8,128)(2,1)} %param.6) | copy-start | bytes 786436
  158.3 166.7 %all-reduce.3.cloned.1.call-start = ((), (), s32[]{:S(2)}) async-start(), calls=%async_computation.6 | async-start | bytes 524288 | tf_op jit(solution)/shard_map/psum | solution.py:60
Sparse Core Ops, SparseCore 0:
  9.9 29.3 all-gather.2
  51.7 50.6 reduce-scatter.2
  104.7 27.2 all-gather.4
  158.4 34.6 reduce-scatter.4
  199.9 124.9 all-reduce.2
where the time goes:
time: 334 us; the launch traced here: 333 us
  waiting for transfers between devices  234 us (70%)
  blocking collectives  30.4 us (9%)
  matrix products  27.4 us (8%)
  local copies, waits for them, and re-layouts  17.1 us (5%)
  between operations  14.6 us (4%)
  other arithmetic  10 us (3%)
    psum x1, waiting for transfers between devices, shards(): lax.psum(weight_terms, ('row', 'col'))  128 us
    reduce_scatter x1, waiting for transfers between devices, shards(): lax.psum_scatter(col_partial, 'row', scatter_dimension=0, tiled=True)  34.8 us
    unnamed x1, blocking collectives  30.4 us
    all_gather x1, waiting for transfers between devices, shards(): col_inputs = lax.all_gather(features, 'row', axis=0, tiled=True)  28.9 us
    all_gather x1, waiting for transfers between devices, shards(): lax.all_gather(grad_sum, 'col', axis=0, tiled=True)  27.2 us
    reduce_scatter x1, waiting for transfers between devices, shards(): lax.psum_scatter(partial_value, 'col', scatter_dimension=0, tiled=True)  14.2 us
    dot_general x1, local copies, waits for them, and re-layouts, shards(): jnp.einsum('bkij,bif->bkjf', tile_bf, grad_slab, preferred_element_type=j...  10.5 us
    dot_general x1, matrix products, shards(): jnp.einsum('bkij,bif->bkjf', tile_bf, grad_slab, preferred_element_type=j...  8.54 us
  transfers between devices with their start and end apart: 5, of which 5 were waited for; matrix products, arithmetic and copies ran while one was open for 3% of the time, Pallas kernels for 0%

commit v1 on v0

v1 whole, which is shorter than its diff:
```python
import functools
import math

import jax
import jax.numpy as jnp
from jax import lax
from jax.experimental import pallas as pl
from jax.experimental.pallas import tpu as pltpu
from jax.sharding import PartitionSpec as P

MESH = pl.DeviceIdType.MESH
BF = jnp.bfloat16
F32 = jnp.float32


def kernel(
    R, C,
    feats, weight, cols, counts, cot, adj,
    out, fgrad, wterm,
    adj_v, dense, hid, deg, deg_rx, part, pair_tx, pair_rx,
    in_r, in_l, tx_r, tx_l, slab, slab_t, ndt, nd_tx, nd_rx,
    adj_sem, h_send, h_recv, d_send, d_recv, p_send, p_recv,
    r_send, r_recv, l_send, l_recv, gr_send, gr_recv, gl_send, gl_recv,
    s_send, s_recv, n_send, n_recv,
):
    r = lax.axis_index("row")
    c = lax.axis_index("col")
    L = C // 2
    z = c // 2
    k = c % 2
    NB, K, T, _ = adj.shape
    O, F = feats.shape
    N = O * R
    J = N // T
    sib = (r, 2 * z + 1 - k)
    right = (r, c + 2)
    left = (r, c - 2)

    def remote(src, dst, ss, rs, dev):
        return pltpu.make_async_remote_copy(
            src_ref=src, dst_ref=dst, send_sem=ss, recv_sem=rs,
            device_id=dev, device_id_type=MESH)

    def row_peer(d):
        return lax.rem(r + d, R)

    def col_peer(d):
        return lax.rem(c + d, C)

    def load_adj(b):
        return pltpu.make_async_copy(adj.at[b], adj_v.at[b], adj_sem.at[b])

    @pl.loop(0, NB)
    def _(b):
        load_adj(b).start()

    barrier = pltpu.get_barrier_semaphore()
    for d in range(1, R):
        pl.semaphore_signal(barrier, inc=1, device_id=(row_peer(d), c), device_id_type=MESH)
    for d in range(1, C):
        pl.semaphore_signal(barrier, inc=1, device_id=(r, col_peer(d)), device_id_type=MESH)

    hid[pl.ds(pl.multiple_of(r * O, O), O), :] = jnp.dot(
        feats[...], weight[...], preferred_element_type=F32).astype(BF)
    pl.semaphore_wait(barrier, R + C - 2)

    def h_copy(d):
        own = hid.at[pl.ds(pl.multiple_of(r * O, O), O), :]
        return remote(own, own, h_send.at[d - 1], h_recv.at[d - 1], (row_peer(d), c))

    for d in range(1, R):
        h_copy(d).start()

    @pl.loop(0, NB)
    def _(b):
        load_adj(b).wait()
        n = counts[b, 0]
        rows = pl.ds(pl.multiple_of(b * T, T), T)
        vals = []
        for s in range(K):
            live = jnp.where(s < n, 1.0, 0.0).astype(F32)
            v = adj_v[b, s].astype(F32) * live
            vals.append(v)
        total = functools.reduce(lambda a, e: a + e, vals)
        deg[:, rows] = lax.dot_general(
            jnp.ones((8, T), BF), total.astype(BF), (((1,), (1,)), ((), ())),
            preferred_element_type=F32)
        for j in range(J):
            acc = None
            for s in range(K):
                m = jnp.where(cols[b, s] == j, 1.0, 0.0).astype(F32)
                term = vals[s] * m
                acc = term if acc is None else acc + term
            dense[rows, j * T:(j + 1) * T] = acc.astype(BF)

    def d_copy(d):
        src = deg.at[:, pl.ds(pl.multiple_of(col_peer(d) * O, O), O)]
        return remote(src, deg_rx.at[d - 1], d_send.at[d - 1], d_recv.at[d - 1],
                      (r, col_peer(d)))

    for d in range(1, C):
        d_copy(d).start()

    for d in range(1, R):
        h_copy(d).wait_recv()

    per = 2 * O // T

    def p_copy(q):
        return remote(pair_tx.at[q], pair_rx.at[q], p_send.at[q], p_recv.at[q], sib)

    def part_of(q, core):
        return pl.ds(pl.multiple_of((2 * q + core) * O, O), O)

    @pl.loop(0, L)
    def _(i):
        q = jnp.where(i % 2 == 0, L - 1 - i // 2, i // 2)
        for bb in range(per):
            rows = pl.ds(pl.multiple_of((q * per + bb) * T, T), T)
            part[rows, :] = jnp.dot(dense[rows, :], hid[...], preferred_element_type=F32)
        pair_tx[q] = part[part_of(q, 1 - k), :].astype(BF)
        p_copy(q).start()

    def r_copy(q):
        return remote(tx_r.at[q], in_r.at[q], r_send.at[q], r_recv.at[q], right)

    def l_copy(q):
        return remote(tx_l.at[q], in_l.at[q], l_send.at[q], l_recv.at[q], left)

    @pl.loop(0, L - 1)
    def _(i):
        qr = L - 1 - i
        ql = i

        @pl.when(qr > z)
        def _():
            p_copy(qr).wait_recv()
            own = part_of(qr, k)
            part[own, :] += pair_rx[qr].astype(F32)

            @pl.when(z > 0)
            def _():
                r_copy(qr).wait_recv()
                part[own, :] += in_r[qr].astype(F32)

            tx_r[qr] = part[own, :].astype(BF)
            r_copy(qr).start()

        @pl.when(ql < z)
        def _():
            p_copy(ql).wait_recv()
            own = part_of(ql, k)
            part[own, :] += pair_rx[ql].astype(F32)

            @pl.when(z < L - 1)
            def _():
                l_copy(ql).wait_recv()
                part[own, :] += in_l[ql].astype(F32)

            tx_l[ql] = part[own, :].astype(BF)
            l_copy(ql).start()

    for d in range(1, C):
        d_copy(d).wait_recv()
    degree = deg[:, pl.ds(pl.multiple_of(c * O, O), O)]
    for d in range(1, C):
        degree = degree + deg_rx[d - 1]
    inv = lax.rsqrt(1.0 + degree)
    inv = jnp.transpose(jnp.broadcast_to(inv[0:1, :], (128, O)))[:, 0:1]

    mine = part_of(z, k)
    p_copy(z).wait_recv()
    part[mine, :] += pair_rx[z].astype(F32)

    @pl.when(z > 0)
    def _():
        r_copy(z).wait_recv()
        part[mine, :] += in_r[z].astype(F32)

    @pl.when(z < L - 1)
    def _():
        l_copy(z).wait_recv()
        part[mine, :] += in_l[z].astype(F32)

    pre = part[mine, :] * inv
    sig = jax.nn.sigmoid(pre)
    out[...] = (pre * sig).astype(BF)
    slab[mine, :] = (cot[...].astype(F32) * sig * (1.0 + pre * (1.0 - sig)) * inv).astype(BF)

    def s_copy(p):
        ref = slab.at[part_of(p, k), :]
        return remote(ref, ref, s_send.at[p], s_recv.at[p], sib)

    def s_wait(p):
        ref = slab.at[part_of(p, 1 - k), :]
        remote(ref, ref, s_send.at[p], s_recv.at[p], sib).wait_recv()

    def gr_copy(i, p):
        ref = slab.at[part_of(p, k), :]
        return remote(ref, ref, gr_send.at[i], gr_recv.at[i], right)

    def gl_copy(i, p):
        ref = slab.at[part_of(p, k), :]
        return remote(ref, ref, gl_send.at[i], gl_recv.at[i], left)

    @pl.when(z < L - 1)
    def _():
        gr_copy(0, z).start()

    @pl.when(z > 0)
    def _():
        gl_copy(0, z).start()

    s_copy(z).start()
    CH = 512 if N % 512 == 0 else T
    ndt[...] = jnp.zeros_like(ndt)

    def accumulate(p):
        rows = pl.ds(pl.multiple_of(2 * p * O, 2 * O), 2 * O)
        slab_t[...] = jnp.transpose(slab[rows, :].astype(F32)).astype(BF)

        @pl.loop(0, N // CH)
        def _(j):
            cc = pl.ds(pl.multiple_of(j * CH, CH), CH)
            ndt[:, cc] += jnp.dot(slab_t[...], dense[rows, cc], preferred_element_type=F32)

    s_wait(z)
    accumulate(z)

    @pl.loop(1, L)
    def _(i):
        pr = z - i
        pln = z + i

        @pl.when(pr >= 0)
        def _():
            gr_copy(i - 1, pr).wait_recv()

            @pl.when(z < L - 1)
            def _():
                gr_copy(i, pr).start()
            s_copy(pr).start()

        @pl.when(pln <= L - 1)
        def _():
            gl_copy(i - 1, pln).wait_recv()

            @pl.when(z > 0)
            def _():
                gl_copy(i, pln).start()
            s_copy(pln).start()

        @pl.when(pr >= 0)
        def _():
            s_wait(pr)
            accumulate(pr)

        @pl.when(pln <= L - 1)
        def _():
            s_wait(pln)
            accumulate(pln)

    def n_copy(d):
        return remote(nd_tx.at[d - 1], nd_rx.at[d - 1], n_send.at[d - 1], n_recv.at[d - 1],
                      (row_peer(d), c))

    for d in range(1, R):
        nd_tx[d - 1] = ndt[:, pl.ds(pl.multiple_of(row_peer(d) * O, O), O)].astype(BF)
        n_copy(d).start()
    total = ndt[:, pl.ds(pl.multiple_of(r * O, O), O)]
    for d in range(1, R):
        n_copy(d).wait_recv()
        total = total + nd_rx[d - 1].astype(F32)
    node = jnp.transpose(total).astype(BF)
    wterm[...] = lax.dot_general(
        feats[...], node, (((0,), (0,)), ((), ())), preferred_element_type=F32)
    fgrad[...] = lax.dot_general(
        node, weight[...], (((1,), (1,)), ((), ())), preferred_element_type=F32).astype(BF)

    for d in range(1, R):
        h_copy(d).wait_send()
        n_copy(d).wait_send()
    for d in range(1, C):
        d_copy(d).wait_send()

    @pl.loop(0, L)
    def _(q):
        p_copy(q).wait_send()
        s_copy(q).wait_send()

        @pl.when(q > z)
        def _():
            r_copy(q).wait_send()

        @pl.when(q < z)
        def _():
            l_copy(q).wait_send()

        @pl.when((q <= z) & (z < L - 1))
        def _():
            gr_copy(q, z - q).wait_send()

        @pl.when((q <= L - 1 - z) & (z > 0))
        def _():
            gl_copy(q, z + q).wait_send()


def shards(features, weight, adjacency, tile_cols, tile_counts, cotangent):
    R = lax.axis_size("row")
    C = lax.axis_size("col")
    L = C // 2
    NB, K, T, _ = adjacency.shape
    O, F = features.shape
    N = O * R
    M = NB * T
    vmem = pl.BlockSpec(memory_space=pltpu.VMEM)
    smem = pl.BlockSpec(memory_space=pltpu.SMEM)
    dma = pltpu.SemaphoreType.DMA
    scratch = [
        pltpu.VMEM((NB, K, T, T), jnp.int32),
        pltpu.VMEM((M, N), BF),
        pltpu.VMEM((N, F), BF),
        pltpu.VMEM((8, M), F32),
        pltpu.VMEM((C - 1, 8, O), F32),
        pltpu.VMEM((M, F), F32),
        pltpu.VMEM((L, O, F), BF),
        pltpu.VMEM((L, O, F), BF),
        pltpu.VMEM((L, O, F), BF),
        pltpu.VMEM((L, O, F), BF),
        pltpu.VMEM((L, O, F), BF),
        pltpu.VMEM((L, O, F), BF),
        pltpu.VMEM((M, F), BF),
        pltpu.VMEM((F, 2 * O), BF),
        pltpu.VMEM((F, N), F32),
        pltpu.VMEM((R - 1, F, O), BF),
        pltpu.VMEM((R - 1, F, O), BF),
        dma((NB,)),
        dma((R - 1,)), dma((R - 1,)),
        dma((C - 1,)), dma((C - 1,)),
        dma((L,)), dma((L,)),
        dma((L,)), dma((L,)),
        dma((L,)), dma((L,)),
        dma((L,)), dma((L,)),
        dma((L,)), dma((L,)),
        dma((L,)), dma((L,)),
        dma((R - 1,)), dma((R - 1,)),
    ]
    out, fgrad, wterm = pl.pallas_call(
        functools.partial(kernel, R, C),
        out_shape=(
            jax.ShapeDtypeStruct((O, F), BF),
            jax.ShapeDtypeStruct((O, F), BF),
            jax.ShapeDtypeStruct((F, F), F32),
        ),
        in_specs=[vmem, vmem, smem, smem, vmem, pl.BlockSpec(memory_space=pl.ANY)],
        out_specs=(vmem, vmem, vmem),
        scratch_shapes=scratch,
        compiler_params=pltpu.CompilerParams(
            collective_id=0, has_side_effects=True, vmem_limit_bytes=60 * 1024 * 1024),
    )(features, weight, tile_cols, tile_counts, cotangent, adjacency)
    node_total = O * R * C
    wgrad = lax.psum(wterm, ("row", "col")) * jnp.float32(1.0 / math.sqrt(node_total))
    return out, fgrad, wgrad


def solution(mesh):
    placed = (
        P(("col", "row"), None),
        P(),
        P("row", "col", None, None),
        P("row", "col"),
        P("row", "col"),
        P(("row", "col"), None),
    )
    return jax.shard_map(
        shards,
        mesh=mesh,
        in_specs=placed,
        out_specs=(P(("row", "col"), None), P(("col", "row"), None), P()),
        check_vma=False,
    )
```

time: 334 us -> 237 us (0.71)
  waiting for transfers between devices: 234 us -> 123 us
  Pallas kernels: 0 us -> 92 us
  blocking collectives: 30.4 us -> 0 us
  matrix products: 27.4 us -> 0 us
  local copies, waits for them, and re-layouts: 17.1 us -> 6.02 us
  other arithmetic: 10 us -> 1.67 us
    pallas_call x0 -> x1, Pallas kernels: none -> 92 us  [shards(): pl.pallas_call(functools.partial(kernel, R, C), out_shape=(jax.ShapeDtype...]
    all_gather x2 -> x0, waiting for transfers between devices: 56.1 us -> none  [the longest x1 28.9 us: shards(): col_inputs = lax.all_gather(features, 'row', axis=0, tiled=True)]
    reduce_scatter x2 -> x0, waiting for transfers between devices: 49 us -> none  [the longest x1 34.8 us: shards(): lax.psum_scatter(col_partial, 'row', scatter_dimension=0, tiled=True)]
    unnamed x1 -> x0, blocking collectives: 30.4 us -> none
    dot_general x6 -> x0, matrix products: 27.4 us -> none  [the longest x1 8.54 us: shards(): jnp.einsum('bkij,bif->bkjf', tile_bf, grad_slab, preferred_element_type=j...]
    dot_general x2 -> x0, local copies, waits for them, and re-layouts: 12.5 us -> none  [the longest x1 10.5 us: shards(): jnp.einsum('bkij,bif->bkjf', tile_bf, grad_slab, preferred_element_type=j...]
    psum x1, waiting for transfers between devices: 128 us -> 122 us  [shards(): lax.psum(wterm, ('row', 'col')) * jnp.float32(1.0 / math.sqrt(node_total))]
    reduce_sum x2 -> x0, other arithmetic: 4.71 us -> none  [the longest x1 4.59 us: shards(): row_sums = jnp.sum(adjacency, axis=3)]
  transfers between devices with their start and end apart: 5 -> 1, of which waited for: 5 -> 1; matrix products, arithmetic and copies ran while one was open for 3% -> 0% of each run, Pallas kernels for 0% -> 0%
where the time goes in v1:
time: 237 us; the launch traced here: 236 us
  waiting for transfers between devices  123 us (52%)
  Pallas kernels  92 us (39%)
  between operations  14 us (6%)
  local copies, waits for them, and re-layouts  6.02 us (3%)
    psum x1, waiting for transfers between devices, shards(): lax.psum(wterm, ('row', 'col')) * jnp.float32(1.0 / math.sqrt(node_total))  122 us
    pallas_call x1, Pallas kernels, shards(): pl.pallas_call(functools.partial(kernel, R, C), out_shape=(jax.ShapeDtype...  92 us
    unnamed x4, local copies, waits for them, and re-layouts  6.02 us
  transfers between devices with their start and end apart: 1, of which 1 were waited for; matrix products, arithmetic and copies ran while one was open for 0% of the time, Pallas kernels for 0%

profile of v1, /device:TPU:0, one launch (start us, length us, event | category | flops | bytes accessed | tf_op | source)
XLA Modules:
  0.0 236.3 jit_solution(5729612718393498441)
XLA Ops:
  7.2 0.0 all-reduce.2.cloned.1.call-start
  7.2 1.4 copy.9.cols
  8.6 1.3 copy.10.counts
  9.9 92.0 %shard_map.85 = (bf16[512,256]{1,0:T(8,128)(2,1)}, bf16[512,256]{1,0:T(8,128)(2,1)}, f32[256,256]{1,0:T(8,128)}) custom-call(bf16[512,256]{1,0:T(8,128)(2,1)} %feats.1, bf16[256,256]{1,0:T(8,128)(2,1)} %weight.1, s32[16,2]{1,0:T(8,128)} %copy.9.cols, s32[16,1]{1,0:T(8,128)} %copy.10.counts, bf16[512,256]{1,0:T(8,128)(2,1)} %cot.1, s32[16,2,256,256]{3,2,1,0:T(8,128)} %adj.1), custom_call_target="tpu_custom_call" | custom-call | tf_op jit(solution)/shard_map/pallas_call | solution.py:348
  101.9 0.0 all-reduce.2.cloned.1.call-update
  101.9 122.5 %all-reduce.2.cloned.1.call-done = f32[256,256]{1,0:T(8,128)} async-done(((f32[256,256]{1,0:T(8,128)}), f32[256,256]{1,0:T(8,128)}) %all-reduce.2.cloned.1.call-update) | async-done | bytes 262160 | tf_op jit(solution)/shard_map/psum | solution.py:362
  224.4 1.7 broadcast_multiply_fusion
  226.1 1.7 copy.14
  227.8 1.7 copy.15
Async XLA Ops:
  7.2 217.2 %all-reduce.2.cloned.1.call-start = ((), (), s32[]{:S(2)}) async-start(), calls=%async_computation | async-start | bytes 524288 | tf_op jit(solution)/shard_map/psum | solution.py:362
Sparse Core Ops, SparseCore 0:
  102.0 122.3 all-reduce.1

commit v2 on v1

--- a/solution.py
+++ b/solution.py
@@ -14,14 +14,16 @@
 
 
 def kernel(
-    R, C,
+    R, C, scale,
     feats, weight, cols, counts, cot, adj,
-    out, fgrad, wterm,
+    out, fgrad, wgrad,
     adj_v, dense, hid, deg, deg_rx, part, pair_tx, pair_rx,
     in_r, in_l, tx_r, tx_l, slab, slab_t, ndt, nd_tx, nd_rx,
+    w_term, w_rx, w_cur, w_in, w_all,
     adj_sem, h_send, h_recv, d_send, d_recv, p_send, p_recv,
     r_send, r_recv, l_send, l_recv, gr_send, gr_recv, gl_send, gl_recv,
     s_send, s_recv, n_send, n_recv,
+    w_send, w_recv, b_send, b_recv, a_send, a_recv,
 ):
     r = lax.axis_index("row")
     c = lax.axis_index("col")
@@ -272,11 +274,54 @@
         n_copy(d).wait_recv()
         total = total + nd_rx[d - 1].astype(F32)
     node = jnp.transpose(total).astype(BF)
-    wterm[...] = lax.dot_general(
+    w_term[...] = lax.dot_general(
         feats[...], node, (((0,), (0,)), ((), ())), preferred_element_type=F32)
+
+    G = F // R
+    steps = C.bit_length() - 1
+
+    def w_rows(i):
+        return pl.ds(pl.multiple_of(i * G, G), G)
+
+    def w_copy(d):
+        return remote(w_term.at[w_rows(row_peer(d)), :], w_rx.at[d - 1],
+                      w_send.at[d - 1], w_recv.at[d - 1], (row_peer(d), c))
+
+    def b_copy(s):
+        w = 1 << s
+        partner = c + w - 2 * w * ((c // w) % 2)
+        return remote(w_cur.at[s], w_in.at[s], b_send.at[s], b_recv.at[s], (r, partner))
+
+    def a_copy(d):
+        ref = w_all.at[w_rows(r), :]
+        return remote(ref, ref, a_send.at[d - 1], a_recv.at[d - 1], (row_peer(d), c))
+
+    for d in range(1, R):
+        w_copy(d).start()
     fgrad[...] = lax.dot_general(
         node, weight[...], (((1,), (1,)), ((), ())), preferred_element_type=F32).astype(BF)
 
+    wsum = w_term[w_rows(r), :]
+    for d in range(1, R):
+        w_copy(d).wait_recv()
+        wsum = wsum + w_rx[d - 1]
+    for s in range(steps):
+        w_cur[s] = wsum
+        b_copy(s).start()
+        b_copy(s).wait_recv()
+        wsum = wsum + w_in[s]
+    w_all[w_rows(r), :] = wsum * scale
+    for d in range(1, R):
+        a_copy(d).start()
+    for d in range(1, R):
+        a_copy(d).wait_recv()
+    wgrad[...] = w_all[...]
+
+    for s in range(steps):
+        b_copy(s).wait_send()
+    for d in range(1, R):
+        w_copy(d).wait_send()
+        a_copy(d).wait_send()
     for d in range(1, R):
         h_copy(d).wait_send()
         n_copy(d).wait_send()
@@ -313,6 +358,9 @@
     O, F = features.shape
     N = O * R
     M = NB * T
+    G = F // R
+    steps = C.bit_length() - 1
+    scale = 1.0 / math.sqrt(O * R * C)
     vmem = pl.BlockSpec(memory_space=pltpu.VMEM)
     smem = pl.BlockSpec(memory_space=pltpu.SMEM)
     dma = pltpu.SemaphoreType.DMA
@@ -334,6 +382,11 @@
         pltpu.VMEM((F, N), F32),
         pltpu.VMEM((R - 1, F, O), BF),
         pltpu.VMEM((R - 1, F, O), BF),
+        pltpu.VMEM((F, F), F32),
+        pltpu.VMEM((R - 1, G, F), F32),
+        pltpu.VMEM((steps, G, F), F32),
+        pltpu.VMEM((steps, G, F), F32),
+        pltpu.VMEM((F, F), F32),
         dma((NB,)),
         dma((R - 1,)), dma((R - 1,)),
         dma((C - 1,)), dma((C - 1,)),
@@ -344,9 +397,12 @@
         dma((L,)), dma((L,)),
         dma((L,)), dma((L,)),
         dma((R - 1,)), dma((R - 1,)),
+        dma((R - 1,)), dma((R - 1,)),
+        dma((steps,)), dma((steps,)),
+        dma((R - 1,)), dma((R - 1,)),
     ]
-    out, fgrad, wterm = pl.pallas_call(
-        functools.partial(kernel, R, C),
+    out, fgrad, wgrad = pl.pallas_call(
+        functools.partial(kernel, R, C, scale),
         out_shape=(
             jax.ShapeDtypeStruct((O, F), BF),
             jax.ShapeDtypeStruct((O, F), BF),
@@ -358,8 +414,6 @@
         compiler_params=pltpu.CompilerParams(
             collective_id=0, has_side_effects=True, vmem_limit_bytes=60 * 1024 * 1024),
     )(features, weight, tile_cols, tile_counts, cotangent, adjacency)
-    node_total = O * R * C
-    wgrad = lax.psum(wterm, ("row", "col")) * jnp.float32(1.0 / math.sqrt(node_total))
     return out, fgrad, wgrad
 
 

time: 237 us -> 116 us (0.49)
  waiting for transfers between devices: 123 us -> 0 us
  Pallas kernels: 92 us -> 107 us
  between operations: 14 us -> 0.64 us
    psum x1 -> x0, waiting for transfers between devices: 122 us -> none  [shards(): lax.psum(wterm, ('row', 'col')) * jnp.float32(1.0 / math.sqrt(node_total))]
    pallas_call x1, Pallas kernels: 92 us -> 107 us  [shards(): pl.pallas_call(functools.partial(kernel, R, C, scale), out_shape=(jax.Sha...]
    unnamed x4 -> x5, local copies, waits for them, and re-layouts: 6.02 us -> 7.69 us
  transfers between devices with their start and end apart: 1 -> 0, of which waited for: 1 -> 0; matrix products, arithmetic and copies ran while one was open for 0% -> 0% of each run, Pallas kernels for 0% -> 0%
where the time goes in v2:
time: 116 us; the launch traced here: 115 us
  Pallas kernels  107 us (92%)
  local copies, waits for them, and re-layouts  7.69 us (7%)
    pallas_call x1, Pallas kernels, shards(): pl.pallas_call(functools.partial(kernel, R, C, scale), out_shape=(jax.Sha...  107 us
    unnamed x5, local copies, waits for them, and re-layouts  7.69 us

profile of v2, /device:TPU:0, one launch (start us, length us, event | category | flops | bytes accessed | tf_op | source)
XLA Modules:
  0.0 115.4 jit_solution(1979461205117389142)
XLA Ops:
  0.6 1.4 %copy.9.cols = s32[16,2]{1,0:T(8,128)} copy(s32[16,2]{0,1:T(2,128)} %param.9) | data formatting | bytes 256 | tf_op args[3]
  2.0 1.3 %copy.10.counts = s32[16,1]{1,0:T(8,128)} copy(s32[16,1]{0,1:T(1,128)} %param.10) | data formatting | bytes 128 | tf_op args[4]
  3.3 107.1 %shard_map.85 = (bf16[512,256]{1,0:T(8,128)(2,1)}, bf16[512,256]{1,0:T(8,128)(2,1)}, f32[256,256]{1,0:T(8,128)}) custom-call(bf16[512,256]{1,0:T(8,128)(2,1)} %feats.1, bf16[256,256]{1,0:T(8,128)(2,1)} %weight.1, s32[16,2]{1,0:T(8,128)} %copy.9.cols, s32[16,1]{1,0:T(8,128)} %copy.10.counts, bf16[512,256]{1,0:T(8,128)(2,1)} %cot.1, s32[16,2,256,256]{3,2,1,0:T(8,128)} %adj.1), custom_call_target="tpu_custom_call" | custom-call | tf_op jit(solution)/shard_map/pallas_call | solution.py:404
  110.4 1.7 %copy.14 = bf16[512,256]{1,0:T(8,128)(2,1)} copy(bf16[512,256]{1,0:T(8,128)(2,1)} %get-tuple-element.6) | data formatting | bytes 524288
  112.1 1.7 %copy.15 = bf16[512,256]{1,0:T(8,128)(2,1)} copy(bf16[512,256]{1,0:T(8,128)(2,1)} %get-tuple-element.7) | data formatting | bytes 524288
  113.8 1.7 %copy.16 = f32[256,256]{1,0:T(8,128)} copy(f32[256,256]{1,0:T(8,128)} %get-tuple-element.8) | data formatting | bytes 524288

commit v3 on v2

--- a/solution.py
+++ b/solution.py
@@ -11,6 +11,7 @@
 MESH = pl.DeviceIdType.MESH
 BF = jnp.bfloat16
 F32 = jnp.float32
+NH = 2
 
 
 def kernel(
@@ -34,6 +35,11 @@
     O, F = feats.shape
     N = O * R
     J = N // T
+    HF = F // NH
+
+    def cs(h):
+        return slice(h * HF, (h + 1) * HF)
+
     sib = (r, 2 * z + 1 - k)
     right = (r, c + 2)
     left = (r, c - 2)
@@ -108,8 +114,9 @@
 
     per = 2 * O // T
 
-    def p_copy(q):
-        return remote(pair_tx.at[q], pair_rx.at[q], p_send.at[q], p_recv.at[q], sib)
+    def p_copy(q, h):
+        return remote(pair_tx.at[q, :, cs(h)], pair_rx.at[q, :, cs(h)],
+                      p_send.at[h, q], p_recv.at[h, q], sib)
 
     def part_of(q, core):
         return pl.ds(pl.multiple_of((2 * q + core) * O, O), O)
@@ -121,46 +128,52 @@
             rows = pl.ds(pl.multiple_of((q * per + bb) * T, T), T)
             part[rows, :] = jnp.dot(dense[rows, :], hid[...], preferred_element_type=F32)
         pair_tx[q] = part[part_of(q, 1 - k), :].astype(BF)
-        p_copy(q).start()
-
-    def r_copy(q):
-        return remote(tx_r.at[q], in_r.at[q], r_send.at[q], r_recv.at[q], right)
-
-    def l_copy(q):
-        return remote(tx_l.at[q], in_l.at[q], l_send.at[q], l_recv.at[q], left)
+        for h in range(NH):
+            p_copy(q, h).start()
+
+    def r_copy(q, h):
+        return remote(tx_r.at[q, :, cs(h)], in_r.at[q, :, cs(h)],
+                      r_send.at[h, q], r_recv.at[h, q], right)
+
+    def l_copy(q, h):
+        return remote(tx_l.at[q, :, cs(h)], in_l.at[q, :, cs(h)],
+                      l_send.at[h, q], l_recv.at[h, q], left)
+
+    def sum_step(i, h):
+        qr = L - 1 - i
+        ql = i
+
+        @pl.when(qr > z)
+        def _():
+            p_copy(qr, h).wait_recv()
+            own = part_of(qr, k)
+            part[own, cs(h)] += pair_rx[qr, :, cs(h)].astype(F32)
+
+            @pl.when(z > 0)
+            def _():
+                r_copy(qr, h).wait_recv()
+                part[own, cs(h)] += in_r[qr, :, cs(h)].astype(F32)
+
+            tx_r[qr, :, cs(h)] = part[own, cs(h)].astype(BF)
+            r_copy(qr, h).start()
+
+        @pl.when(ql < z)
+        def _():
+            p_copy(ql, h).wait_recv()
+            own = part_of(ql, k)
+            part[own, cs(h)] += pair_rx[ql, :, cs(h)].astype(F32)
+
+            @pl.when(z < L - 1)
+            def _():
+                l_copy(ql, h).wait_recv()
+                part[own, cs(h)] += in_l[ql, :, cs(h)].astype(F32)
+
+            tx_l[ql, :, cs(h)] = part[own, cs(h)].astype(BF)
+            l_copy(ql, h).start()
 
     @pl.loop(0, L - 1)
     def _(i):
-        qr = L - 1 - i
-        ql = i
-
-        @pl.when(qr > z)
-        def _():
-            p_copy(qr).wait_recv()
-            own = part_of(qr, k)
-            part[own, :] += pair_rx[qr].astype(F32)
-
-            @pl.when(z > 0)
-            def _():
-                r_copy(qr).wait_recv()
-                part[own, :] += in_r[qr].astype(F32)
-
-            tx_r[qr] = part[own, :].astype(BF)
-            r_copy(qr).start()
-
-        @pl.when(ql < z)
-        def _():
-            p_copy(ql).wait_recv()
-            own = part_of(ql, k)
-            part[own, :] += pair_rx[ql].astype(F32)
-
-            @pl.when(z < L - 1)
-            def _():
-                l_copy(ql).wait_recv()
-                part[own, :] += in_l[ql].astype(F32)
-
-            tx_l[ql] = part[own, :].astype(BF)
-            l_copy(ql).start()
+        sum_step(i, 0)
 
     for d in range(1, C):
         d_copy(d).wait_recv()
@@ -171,107 +184,141 @@
     inv = jnp.transpose(jnp.broadcast_to(inv[0:1, :], (128, O)))[:, 0:1]
 
     mine = part_of(z, k)
-    p_copy(z).wait_recv()
-    part[mine, :] += pair_rx[z].astype(F32)
-
-    @pl.when(z > 0)
-    def _():
-        r_copy(z).wait_recv()
-        part[mine, :] += in_r[z].astype(F32)
-
-    @pl.when(z < L - 1)
-    def _():
-        l_copy(z).wait_recv()
-        part[mine, :] += in_l[z].astype(F32)
-
-    pre = part[mine, :] * inv
-    sig = jax.nn.sigmoid(pre)
-    out[...] = (pre * sig).astype(BF)
-    slab[mine, :] = (cot[...].astype(F32) * sig * (1.0 + pre * (1.0 - sig)) * inv).astype(BF)
-
-    def s_copy(p):
-        ref = slab.at[part_of(p, k), :]
-        return remote(ref, ref, s_send.at[p], s_recv.at[p], sib)
-
-    def s_wait(p):
-        ref = slab.at[part_of(p, 1 - k), :]
-        remote(ref, ref, s_send.at[p], s_recv.at[p], sib).wait_recv()
-
-    def gr_copy(i, p):
-        ref = slab.at[part_of(p, k), :]
-        return remote(ref, ref, gr_send.at[i], gr_recv.at[i], right)
-
-    def gl_copy(i, p):
-        ref = slab.at[part_of(p, k), :]
-        return remote(ref, ref, gl_send.at[i], gl_recv.at[i], left)
-
-    @pl.when(z < L - 1)
-    def _():
-        gr_copy(0, z).start()
-
-    @pl.when(z > 0)
-    def _():
-        gl_copy(0, z).start()
-
-    s_copy(z).start()
+
+    def finish(h):
+        p_copy(z, h).wait_recv()
+        part[mine, cs(h)] += pair_rx[z, :, cs(h)].astype(F32)
+
+        @pl.when(z > 0)
+        def _():
+            r_copy(z, h).wait_recv()
+            part[mine, cs(h)] += in_r[z, :, cs(h)].astype(F32)
+
+        @pl.when(z < L - 1)
+        def _():
+            l_copy(z, h).wait_recv()
+            part[mine, cs(h)] += in_l[z, :, cs(h)].astype(F32)
+
+        pre = part[mine, cs(h)] * inv
+        sig = jax.nn.sigmoid(pre)
+        out[:, cs(h)] = (pre * sig).astype(BF)
+        slab[mine, cs(h)] = (
+            cot[:, cs(h)].astype(F32) * sig * (1.0 + pre * (1.0 - sig)) * inv).astype(BF)
+
+    def s_copy(p, h):
+        ref = slab.at[part_of(p, k), cs(h)]
+        return remote(ref, ref, s_send.at[h, p], s_recv.at[h, p], sib)
+
+    def s_wait(p, h):
+        ref = slab.at[part_of(p, 1 - k), cs(h)]
+        remote(ref, ref, s_send.at[h, p], s_recv.at[h, p], sib).wait_recv()
+
+    def gr_copy(i, p, h):
+        ref = slab.at[part_of(p, k), cs(h)]
+        return remote(ref, ref, gr_send.at[h, i], gr_recv.at[h, i], right)
+
+    def gl_copy(i, p, h):
+        ref = slab.at[part_of(p, k), cs(h)]
+        return remote(ref, ref, gl_send.at[h, i], gl_recv.at[h, i], left)
+
+    def spread(h):
+        @pl.when(z < L - 1)
+        def _():
+            gr_copy(0, z, h).start()
+
+        @pl.when(z > 0)
+        def _():
+            gl_copy(0, z, h).start()
+
+        s_copy(z, h).start()
+
+    def forward(i, h):
+        pr = z - i
+        pln = z + i
+
+        @pl.when(pr >= 0)
+        def _():
+            gr_copy(i - 1, pr, h).wait_recv()
+
+            @pl.when(z < L - 1)
+            def _():
+                gr_copy(i, pr, h).start()
+            s_copy(pr, h).start()
+
+        @pl.when(pln <= L - 1)
+        def _():
+            gl_copy(i - 1, pln, h).wait_recv()
+
+            @pl.when(z > 0)
+            def _():
+                gl_copy(i, pln, h).start()
+            s_copy(pln, h).start()
+
     CH = 512 if N % 512 == 0 else T
-    ndt[...] = jnp.zeros_like(ndt)
-
-    def accumulate(p):
+
+    def accumulate(p, h, first=False):
         rows = pl.ds(pl.multiple_of(2 * p * O, 2 * O), 2 * O)
-        slab_t[...] = jnp.transpose(slab[rows, :].astype(F32)).astype(BF)
+        s_wait(p, h)
+        slab_t[...] = jnp.transpose(slab[rows, cs(h)].astype(F32)).astype(BF)
 
         @pl.loop(0, N // CH)
         def _(j):
             cc = pl.ds(pl.multiple_of(j * CH, CH), CH)
-            ndt[:, cc] += jnp.dot(slab_t[...], dense[rows, cc], preferred_element_type=F32)
-
-    s_wait(z)
-    accumulate(z)
+            term = jnp.dot(slab_t[...], dense[rows, cc], preferred_element_type=F32)
+            if first:
+                ndt[cs(h), cc] = term
+            else:
+                ndt[cs(h), cc] += term
+
+    def both(i, h):
+        @pl.when(z - i >= 0)
+        def _():
+            accumulate(z - i, h)
+
+        @pl.when(z + i <= L - 1)
+        def _():
+            accumulate(z + i, h)
+
+    def n_copy(d, h):
+        return remote(nd_tx.at[d - 1, cs(h), :], nd_rx.at[d - 1, cs(h), :],
+                      n_send.at[h, d - 1], n_recv.at[h, d - 1], (row_peer(d), c))
+
+    def scatter(h):
+        for d in range(1, R):
+            there = pl.ds(pl.multiple_of(row_peer(d) * O, O), O)
+            nd_tx[d - 1, cs(h), :] = ndt[cs(h), there].astype(BF)
+            n_copy(d, h).start()
+
+    finish(0)
+    spread(0)
+
+    @pl.loop(0, L - 1)
+    def _(i):
+        sum_step(i, 1)
+        forward(i + 1, 0)
+
+    finish(1)
+    spread(1)
+    accumulate(z, 0, True)
 
     @pl.loop(1, L)
     def _(i):
-        pr = z - i
-        pln = z + i
-
-        @pl.when(pr >= 0)
-        def _():
-            gr_copy(i - 1, pr).wait_recv()
-
-            @pl.when(z < L - 1)
-            def _():
-                gr_copy(i, pr).start()
-            s_copy(pr).start()
-
-        @pl.when(pln <= L - 1)
-        def _():
-            gl_copy(i - 1, pln).wait_recv()
-
-            @pl.when(z > 0)
-            def _():
-                gl_copy(i, pln).start()
-            s_copy(pln).start()
-
-        @pl.when(pr >= 0)
-        def _():
-            s_wait(pr)
-            accumulate(pr)
-
-        @pl.when(pln <= L - 1)
-        def _():
-            s_wait(pln)
-            accumulate(pln)
-
-    def n_copy(d):
-        return remote(nd_tx.at[d - 1], nd_rx.at[d - 1], n_send.at[d - 1], n_recv.at[d - 1],
-                      (row_peer(d), c))
-
-    for d in range(1, R):
-        nd_tx[d - 1] = ndt[:, pl.ds(pl.multiple_of(row_peer(d) * O, O), O)].astype(BF)
-        n_copy(d).start()
+        forward(i, 1)
+        both(i, 0)
+
+    scatter(0)
+    accumulate(z, 1, True)
+
+    @pl.loop(1, L)
+    def _(i):
+        both(i, 1)
+
+    scatter(1)
+
     total = ndt[:, pl.ds(pl.multiple_of(r * O, O), O)]
     for d in range(1, R):
-        n_copy(d).wait_recv()
+        for h in range(NH):
+            n_copy(d, h).wait_recv()
         total = total + nd_rx[d - 1].astype(F32)
     node = jnp.transpose(total).astype(BF)
     w_term[...] = lax.dot_general(
@@ -317,6 +364,26 @@
         a_copy(d).wait_recv()
     wgrad[...] = w_all[...]
 
+    def drain(q, h):
+        p_copy(q, h).wait_send()
+        s_copy(q, h).wait_send()
+
+        @pl.when(q > z)
+        def _():
+            r_copy(q, h).wait_send()
+
+        @pl.when(q < z)
+        def _():
+            l_copy(q, h).wait_send()
+
+        @pl.when((q <= z) & (z < L - 1))
+        def _():
+            gr_copy(q, z - q, h).wait_send()
+
+        @pl.when((q <= L - 1 - z) & (z > 0))
+        def _():
+            gl_copy(q, z + q, h).wait_send()
+
     for s in range(steps):
         b_copy(s).wait_send()
     for d in range(1, R):
@@ -324,30 +391,15 @@
         a_copy(d).wait_send()
     for d in range(1, R):
         h_copy(d).wait_send()
-        n_copy(d).wait_send()
+        for h in range(NH):
+            n_copy(d, h).wait_send()
     for d in range(1, C):
         d_copy(d).wait_send()
 
     @pl.loop(0, L)
     def _(q):
-        p_copy(q).wait_send()
-        s_copy(q).wait_send()
-
-        @pl.when(q > z)
-        def _():
-            r_copy(q).wait_send()
-
-        @pl.when(q < z)
-        def _():
-            l_copy(q).wait_send()
-
-        @pl.when((q <= z) & (z < L - 1))
-        def _():
-            gr_copy(q, z - q).wait_send()
-
-        @pl.when((q <= L - 1 - z) & (z > 0))
-        def _():
-            gl_copy(q, z + q).wait_send()
+        for h in range(NH):
+            drain(q, h)
 
 
 def shards(features, weight, adjacency, tile_cols, tile_counts, cotangent):
@@ -378,7 +430,7 @@
         pltpu.VMEM((L, O, F), BF),
         pltpu.VMEM((L, O, F), BF),
         pltpu.VMEM((M, F), BF),
-        pltpu.VMEM((F, 2 * O), BF),
+        pltpu.VMEM((F // NH, 2 * O), BF),
         pltpu.VMEM((F, N), F32),
         pltpu.VMEM((R - 1, F, O), BF),
         pltpu.VMEM((R - 1, F, O), BF),
@@ -390,13 +442,13 @@
         dma((NB,)),
         dma((R - 1,)), dma((R - 1,)),
         dma((C - 1,)), dma((C - 1,)),
-        dma((L,)), dma((L,)),
-        dma((L,)), dma((L,)),
-        dma((L,)), dma((L,)),
-        dma((L,)), dma((L,)),
-        dma((L,)), dma((L,)),
-        dma((L,)), dma((L,)),
-        dma((R - 1,)), dma((R - 1,)),
+        dma((NH, L)), dma((NH, L)),
+        dma((NH, L)), dma((NH, L)),
+        dma((NH, L)), dma((NH, L)),
+        dma((NH, L)), dma((NH, L)),
+        dma((NH, L)), dma((NH, L)),
+        dma((NH, L)), dma((NH, L)),
+        dma((NH, R - 1)), dma((NH, R - 1)),
         dma((R - 1,)), dma((R - 1,)),
         dma((steps,)), dma((steps,)),
         dma((R - 1,)), dma((R - 1,)),

time: 116 us -> 123 us (1.060)
  Pallas kernels: 107 us -> 114 us
    pallas_call x1, Pallas kernels: 107 us -> 114 us  [shards(): pl.pallas_call(functools.partial(kernel, R, C, scale), out_shape=(jax.Sha...]
where the time goes in v3:
time: 123 us; the launch traced here: 122 us
  Pallas kernels  114 us (93%)
  local copies, waits for them, and re-layouts  7.69 us (6%)
    pallas_call x1, Pallas kernels, shards(): pl.pallas_call(functools.partial(kernel, R, C, scale), out_shape=(jax.Sha...  114 us
    unnamed x5, local copies, waits for them, and re-layouts  7.69 us

profile of v3, /device:TPU:0, one launch (start us, length us, event | category | flops | bytes accessed | tf_op | source)
XLA Modules:
  0.0 122.4 jit_solution(7673627000101669074)
XLA Ops:
  0.6 1.4 %copy.9.cols = s32[16,2]{1,0:T(8,128)} copy(s32[16,2]{0,1:T(2,128)} %param.9) | data formatting | bytes 256 | tf_op args[3]
  2.0 1.3 %copy.10.counts = s32[16,1]{1,0:T(8,128)} copy(s32[16,1]{0,1:T(1,128)} %param.10) | data formatting | bytes 128 | tf_op args[4]
  3.3 114.1 %shard_map.85 = (bf16[512,256]{1,0:T(8,128)(2,1)}, bf16[512,256]{1,0:T(8,128)(2,1)}, f32[256,256]{1,0:T(8,128)}) custom-call(bf16[512,256]{1,0:T(8,128)(2,1)} %feats.1, bf16[256,256]{1,0:T(8,128)(2,1)} %weight.1, s32[16,2]{1,0:T(8,128)} %copy.9.cols, s32[16,1]{1,0:T(8,128)} %copy.10.counts, bf16[512,256]{1,0:T(8,128)(2,1)} %cot.1, s32[16,2,256,256]{3,2,1,0:T(8,128)} %adj.1), custom_call_target="tpu_custom_call" | custom-call | tf_op jit(solution)/shard_map/pallas_call | solution.py:456
  117.4 1.7 %copy.14 = bf16[512,256]{1,0:T(8,128)(2,1)} copy(bf16[512,256]{1,0:T(8,128)(2,1)} %get-tuple-element.6) | data formatting | bytes 524288
  119.1 1.7 %copy.15 = bf16[512,256]{1,0:T(8,128)(2,1)} copy(bf16[512,256]{1,0:T(8,128)(2,1)} %get-tuple-element.7) | data formatting | bytes 524288
  120.7 1.7 %copy.16 = f32[256,256]{1,0:T(8,128)} copy(f32[256,256]{1,0:T(8,128)} %get-tuple-element.8) | data formatting | bytes 524288

commit v4 on v3

--- a/solution.py
+++ b/solution.py
@@ -115,7 +115,7 @@
     per = 2 * O // T
 
     def p_copy(q, h):
-        return remote(pair_tx.at[q, :, cs(h)], pair_rx.at[q, :, cs(h)],
+        return remote(pair_tx.at[h, q], pair_rx.at[h, q],
                       p_send.at[h, q], p_recv.at[h, q], sib)
 
     def part_of(q, core):
@@ -127,16 +127,16 @@
         for bb in range(per):
             rows = pl.ds(pl.multiple_of((q * per + bb) * T, T), T)
             part[rows, :] = jnp.dot(dense[rows, :], hid[...], preferred_element_type=F32)
-        pair_tx[q] = part[part_of(q, 1 - k), :].astype(BF)
         for h in range(NH):
+            pair_tx[h, q] = part[part_of(q, 1 - k), cs(h)].astype(BF)
             p_copy(q, h).start()
 
     def r_copy(q, h):
-        return remote(tx_r.at[q, :, cs(h)], in_r.at[q, :, cs(h)],
+        return remote(tx_r.at[h, q], in_r.at[h, q],
                       r_send.at[h, q], r_recv.at[h, q], right)
 
     def l_copy(q, h):
-        return remote(tx_l.at[q, :, cs(h)], in_l.at[q, :, cs(h)],
+        return remote(tx_l.at[h, q], in_l.at[h, q],
                       l_send.at[h, q], l_recv.at[h, q], left)
 
     def sum_step(i, h):
@@ -147,28 +147,28 @@
         def _():
             p_copy(qr, h).wait_recv()
             own = part_of(qr, k)
-            part[own, cs(h)] += pair_rx[qr, :, cs(h)].astype(F32)
+            part[own, cs(h)] += pair_rx[h, qr].astype(F32)
 
             @pl.when(z > 0)
             def _():
                 r_copy(qr, h).wait_recv()
-                part[own, cs(h)] += in_r[qr, :, cs(h)].astype(F32)
-
-            tx_r[qr, :, cs(h)] = part[own, cs(h)].astype(BF)
+                part[own, cs(h)] += in_r[h, qr].astype(F32)
+
+            tx_r[h, qr] = part[own, cs(h)].astype(BF)
             r_copy(qr, h).start()
 
         @pl.when(ql < z)
         def _():
             p_copy(ql, h).wait_recv()
             own = part_of(ql, k)
-            part[own, cs(h)] += pair_rx[ql, :, cs(h)].astype(F32)
+            part[own, cs(h)] += pair_rx[h, ql].astype(F32)
 
             @pl.when(z < L - 1)
             def _():
                 l_copy(ql, h).wait_recv()
-                part[own, cs(h)] += in_l[ql, :, cs(h)].astype(F32)
-
-            tx_l[ql, :, cs(h)] = part[own, cs(h)].astype(BF)
+                part[own, cs(h)] += in_l[h, ql].astype(F32)
+
+            tx_l[h, ql] = part[own, cs(h)].astype(BF)
             l_copy(ql, h).start()
 
     @pl.loop(0, L - 1)
@@ -187,38 +187,38 @@
 
     def finish(h):
         p_copy(z, h).wait_recv()
-        part[mine, cs(h)] += pair_rx[z, :, cs(h)].astype(F32)
+        part[mine, cs(h)] += pair_rx[h, z].astype(F32)
 
         @pl.when(z > 0)
         def _():
             r_copy(z, h).wait_recv()
-            part[mine, cs(h)] += in_r[z, :, cs(h)].astype(F32)
+            part[mine, cs(h)] += in_r[h, z].astype(F32)
 
         @pl.when(z < L - 1)
         def _():
             l_copy(z, h).wait_recv()
-            part[mine, cs(h)] += in_l[z, :, cs(h)].astype(F32)
+            part[mine, cs(h)] += in_l[h, z].astype(F32)
 
         pre = part[mine, cs(h)] * inv
         sig = jax.nn.sigmoid(pre)
         out[:, cs(h)] = (pre * sig).astype(BF)
-        slab[mine, cs(h)] = (
+        slab[h, mine, :] = (
             cot[:, cs(h)].astype(F32) * sig * (1.0 + pre * (1.0 - sig)) * inv).astype(BF)
 
     def s_copy(p, h):
-        ref = slab.at[part_of(p, k), cs(h)]
+        ref = slab.at[h, part_of(p, k), :]
         return remote(ref, ref, s_send.at[h, p], s_recv.at[h, p], sib)
 
     def s_wait(p, h):
-        ref = slab.at[part_of(p, 1 - k), cs(h)]
+        ref = slab.at[h, part_of(p, 1 - k), :]
         remote(ref, ref, s_send.at[h, p], s_recv.at[h, p], sib).wait_recv()
 
     def gr_copy(i, p, h):
-        ref = slab.at[part_of(p, k), cs(h)]
+        ref = slab.at[h, part_of(p, k), :]
         return remote(ref, ref, gr_send.at[h, i], gr_recv.at[h, i], right)
 
     def gl_copy(i, p, h):
-        ref = slab.at[part_of(p, k), cs(h)]
+        ref = slab.at[h, part_of(p, k), :]
         return remote(ref, ref, gl_send.at[h, i], gl_recv.at[h, i], left)
 
     def spread(h):
@@ -259,7 +259,7 @@
     def accumulate(p, h, first=False):
         rows = pl.ds(pl.multiple_of(2 * p * O, 2 * O), 2 * O)
         s_wait(p, h)
-        slab_t[...] = jnp.transpose(slab[rows, cs(h)].astype(F32)).astype(BF)
+        slab_t[...] = jnp.transpose(slab[h, rows, :].astype(F32)).astype(BF)
 
         @pl.loop(0, N // CH)
         def _(j):
@@ -423,13 +423,13 @@
         pltpu.VMEM((8, M), F32),
         pltpu.VMEM((C - 1, 8, O), F32),
         pltpu.VMEM((M, F), F32),
-        pltpu.VMEM((L, O, F), BF),
-        pltpu.VMEM((L, O, F), BF),
-        pltpu.VMEM((L, O, F), BF),
-        pltpu.VMEM((L, O, F), BF),
-        pltpu.VMEM((L, O, F), BF),
-        pltpu.VMEM((L, O, F), BF),
-        pltpu.VMEM((M, F), BF),
+        pltpu.VMEM((NH, L, O, F // NH), BF),
+        pltpu.VMEM((NH, L, O, F // NH), BF),
+        pltpu.VMEM((NH, L, O, F // NH), BF),
+        pltpu.VMEM((NH, L, O, F // NH), BF),
+        pltpu.VMEM((NH, L, O, F // NH), BF),
+        pltpu.VMEM((NH, L, O, F // NH), BF),
+        pltpu.VMEM((NH, M, F // NH), BF),
         pltpu.VMEM((F // NH, 2 * O), BF),
         pltpu.VMEM((F, N), F32),
         pltpu.VMEM((R - 1, F, O), BF),

time: 123 us -> 123 us (level)
  no operation moved by 1% of the time
where the time goes in v4:
time: 123 us; the launch traced here: 122 us
  Pallas kernels  114 us (93%)
  local copies, waits for them, and re-layouts  7.69 us (6%)
    pallas_call x1, Pallas kernels, shards(): pl.pallas_call(functools.partial(kernel, R, C, scale), out_shape=(jax.Sha...  114 us
    unnamed x5, local copies, waits for them, and re-layouts  7.69 us

profile of v4, /device:TPU:0, one launch (start us, length us, event | category | flops | bytes accessed | tf_op | source)
XLA Modules:
  0.0 122.3 jit_solution(9232550648238908896)
XLA Ops:
  0.6 1.4 %copy.9.cols = s32[16,2]{1,0:T(8,128)} copy(s32[16,2]{0,1:T(2,128)} %param.9) | data formatting | bytes 256 | tf_op args[3]
  2.0 1.3 %copy.10.counts = s32[16,1]{1,0:T(8,128)} copy(s32[16,1]{0,1:T(1,128)} %param.10) | data formatting | bytes 128 | tf_op args[4]
  3.3 114.0 %shard_map.85 = (bf16[512,256]{1,0:T(8,128)(2,1)}, bf16[512,256]{1,0:T(8,128)(2,1)}, f32[256,256]{1,0:T(8,128)}) custom-call(bf16[512,256]{1,0:T(8,128)(2,1)} %feats.1, bf16[256,256]{1,0:T(8,128)(2,1)} %weight.1, s32[16,2]{1,0:T(8,128)} %copy.9.cols, s32[16,1]{1,0:T(8,128)} %copy.10.counts, bf16[512,256]{1,0:T(8,128)(2,1)} %cot.1, s32[16,2,256,256]{3,2,1,0:T(8,128)} %adj.1), custom_call_target="tpu_custom_call" | custom-call | tf_op jit(solution)/shard_map/pallas_call | solution.py:456
  117.3 1.7 %copy.14 = bf16[512,256]{1,0:T(8,128)(2,1)} copy(bf16[512,256]{1,0:T(8,128)(2,1)} %get-tuple-element.6) | data formatting | bytes 524288
  119.0 1.7 %copy.15 = bf16[512,256]{1,0:T(8,128)(2,1)} copy(bf16[512,256]{1,0:T(8,128)(2,1)} %get-tuple-element.7) | data formatting | bytes 524288
  120.6 1.7 %copy.16 = f32[256,256]{1,0:T(8,128)} copy(f32[256,256]{1,0:T(8,128)} %get-tuple-element.8) | data formatting | bytes 524288

commit v5 on v2

--- a/solution.py
+++ b/solution.py
@@ -19,7 +19,7 @@
     out, fgrad, wgrad,
     adj_v, dense, hid, deg, deg_rx, part, pair_tx, pair_rx,
     in_r, in_l, tx_r, tx_l, slab, slab_t, ndt, nd_tx, nd_rx,
-    w_term, w_rx, w_cur, w_in, w_all,
+    w_term, w_tx, w_rx, w_cur, w_in, w_all,
     adj_sem, h_send, h_recv, d_send, d_recv, p_send, p_recv,
     r_send, r_recv, l_send, l_recv, gr_send, gr_recv, gl_send, gl_recv,
     s_send, s_recv, n_send, n_recv,
@@ -284,7 +284,7 @@
         return pl.ds(pl.multiple_of(i * G, G), G)
 
     def w_copy(d):
-        return remote(w_term.at[w_rows(row_peer(d)), :], w_rx.at[d - 1],
+        return remote(w_tx.at[w_rows(row_peer(d)), :], w_rx.at[d - 1],
                       w_send.at[d - 1], w_recv.at[d - 1], (row_peer(d), c))
 
     def b_copy(s):
@@ -296,6 +296,7 @@
         ref = w_all.at[w_rows(r), :]
         return remote(ref, ref, a_send.at[d - 1], a_recv.at[d - 1], (row_peer(d), c))
 
+    w_tx[...] = w_term[...].astype(BF)
     for d in range(1, R):
         w_copy(d).start()
     fgrad[...] = lax.dot_general(
@@ -304,7 +305,7 @@
     wsum = w_term[w_rows(r), :]
     for d in range(1, R):
         w_copy(d).wait_recv()
-        wsum = wsum + w_rx[d - 1]
+        wsum = wsum + w_rx[d - 1].astype(F32)
     for s in range(steps):
         w_cur[s] = wsum
         b_copy(s).start()
@@ -383,7 +384,8 @@
         pltpu.VMEM((R - 1, F, O), BF),
         pltpu.VMEM((R - 1, F, O), BF),
         pltpu.VMEM((F, F), F32),
-        pltpu.VMEM((R - 1, G, F), F32),
+        pltpu.VMEM((F, F), BF),
+        pltpu.VMEM((R - 1, G, F), BF),
         pltpu.VMEM((steps, G, F), F32),
         pltpu.VMEM((steps, G, F), F32),
         pltpu.VMEM((F, F), F32),

time: 116 us -> 114 us (0.983)
    pallas_call x1, Pallas kernels: 107 us -> 106 us  [shards(): pl.pallas_call(functools.partial(kernel, R, C, scale), out_shape=(jax.Sha...]
where the time goes in v5:
time: 114 us
  Pallas kernels  106 us (93%)
  local copies, waits for them, and re-layouts  7.69 us (7%)
    pallas_call x1, Pallas kernels, shards(): pl.pallas_call(functools.partial(kernel, R, C, scale), out_shape=(jax.Sha...  106 us
    unnamed x5, local copies, waits for them, and re-layouts  7.69 us

profile of v5, /device:TPU:0, one launch (start us, length us, event | category | flops | bytes accessed | tf_op | source)
XLA Modules:
  0.0 113.9 jit_solution(11492190523004722742)
XLA Ops:
  0.6 1.4 %copy.9.cols = s32[16,2]{1,0:T(8,128)} copy(s32[16,2]{0,1:T(2,128)} %param.9) | data formatting | bytes 256 | tf_op args[3]
  2.0 1.3 %copy.10.counts = s32[16,1]{1,0:T(8,128)} copy(s32[16,1]{0,1:T(1,128)} %param.10) | data formatting | bytes 128 | tf_op args[4]
  3.3 105.6 %shard_map.85 = (bf16[512,256]{1,0:T(8,128)(2,1)}, bf16[512,256]{1,0:T(8,128)(2,1)}, f32[256,256]{1,0:T(8,128)}) custom-call(bf16[512,256]{1,0:T(8,128)(2,1)} %feats.1, bf16[256,256]{1,0:T(8,128)(2,1)} %weight.1, s32[16,2]{1,0:T(8,128)} %copy.9.cols, s32[16,1]{1,0:T(8,128)} %copy.10.counts, bf16[512,256]{1,0:T(8,128)(2,1)} %cot.1, s32[16,2,256,256]{3,2,1,0:T(8,128)} %adj.1), custom_call_target="tpu_custom_call" | custom-call | tf_op jit(solution)/shard_map/pallas_call | solution.py:406
  108.9 1.7 %copy.14 = bf16[512,256]{1,0:T(8,128)(2,1)} copy(bf16[512,256]{1,0:T(8,128)(2,1)} %get-tuple-element.6) | data formatting | bytes 524288
  110.6 1.7 %copy.15 = bf16[512,256]{1,0:T(8,128)(2,1)} copy(bf16[512,256]{1,0:T(8,128)(2,1)} %get-tuple-element.7) | data formatting | bytes 524288
  112.2 1.7 %copy.16 = f32[256,256]{1,0:T(8,128)} copy(f32[256,256]{1,0:T(8,128)} %get-tuple-element.8) | data formatting | bytes 524288

commit v6 on v5

--- a/solution.py
+++ b/solution.py
@@ -311,12 +311,12 @@
         b_copy(s).start()
         b_copy(s).wait_recv()
         wsum = wsum + w_in[s]
-    w_all[w_rows(r), :] = wsum * scale
+    w_all[w_rows(r), :] = (wsum * scale).astype(BF)
     for d in range(1, R):
         a_copy(d).start()
     for d in range(1, R):
         a_copy(d).wait_recv()
-    wgrad[...] = w_all[...]
+    wgrad[...] = w_all[...].astype(F32)
 
     for s in range(steps):
         b_copy(s).wait_send()
@@ -388,7 +388,7 @@
         pltpu.VMEM((R - 1, G, F), BF),
         pltpu.VMEM((steps, G, F), F32),
         pltpu.VMEM((steps, G, F), F32),
-        pltpu.VMEM((F, F), F32),
+        pltpu.VMEM((F, F), BF),
         dma((NB,)),
         dma((R - 1,)), dma((R - 1,)),
         dma((C - 1,)), dma((C - 1,)),

time: 114 us -> 113 us (level)
  no operation moved by 1% of the time
where the time goes in v6:
time: 113 us
  Pallas kernels  105 us (93%)
  local copies, waits for them, and re-layouts  7.69 us (7%)
    pallas_call x1, Pallas kernels, shards(): pl.pallas_call(functools.partial(kernel, R, C, scale), out_shape=(jax.Sha...  105 us
    unnamed x5, local copies, waits for them, and re-layouts  7.69 us

profile of v6, /device:TPU:0, one launch (start us, length us, event | category | flops | bytes accessed | tf_op | source)
XLA Modules:
  0.0 113.2 jit_solution(368283858160632087)
XLA Ops:
  0.6 1.4 %copy.9.cols = s32[16,2]{1,0:T(8,128)} copy(s32[16,2]{0,1:T(2,128)} %param.9) | data formatting | bytes 256 | tf_op args[3]
  2.0 1.3 %copy.10.counts = s32[16,1]{1,0:T(8,128)} copy(s32[16,1]{0,1:T(1,128)} %param.10) | data formatting | bytes 128 | tf_op args[4]
  3.3 104.9 %shard_map.85 = (bf16[512,256]{1,0:T(8,128)(2,1)}, bf16[512,256]{1,0:T(8,128)(2,1)}, f32[256,256]{1,0:T(8,128)}) custom-call(bf16[512,256]{1,0:T(8,128)(2,1)} %feats.1, bf16[256,256]{1,0:T(8,128)(2,1)} %weight.1, s32[16,2]{1,0:T(8,128)} %copy.9.cols, s32[16,1]{1,0:T(8,128)} %copy.10.counts, bf16[512,256]{1,0:T(8,128)(2,1)} %cot.1, s32[16,2,256,256]{3,2,1,0:T(8,128)} %adj.1), custom_call_target="tpu_custom_call" | custom-call | tf_op jit(solution)/shard_map/pallas_call | solution.py:406
  108.2 1.7 %copy.14 = bf16[512,256]{1,0:T(8,128)(2,1)} copy(bf16[512,256]{1,0:T(8,128)(2,1)} %get-tuple-element.6) | data formatting | bytes 524288
  109.9 1.7 %copy.15 = bf16[512,256]{1,0:T(8,128)(2,1)} copy(bf16[512,256]{1,0:T(8,128)(2,1)} %get-tuple-element.7) | data formatting | bytes 524288
  111.5 1.7 %copy.16 = f32[256,256]{1,0:T(8,128)} copy(f32[256,256]{1,0:T(8,128)} %get-tuple-element.8) | data formatting | bytes 524288
